TPU v7x, 32 devices: a whole 2x2x4 slice. The times are simulated.
32 devices in a mesh: dm: 16 (over z, y, x), chan: 2 (over core).
Axes of the slice: x: 2, y: 2, z: 4, core: 2. Of those that a mesh axis runs over, the one named last changes fastest.
Arguments:
- phased: bfloat16 [16, 256, 2, 4096], P('dm', None, None, 'chan')
- filters: bfloat16 [32, 4096, 512], P('dm', 'chan'), may hold values from -0.375 to 0.375
- tap_blocks: int32 [32], replicated, may hold values from 1 to 4, as said below
- stretch_owner: int32 [4], replicated, may hold values from 0 to 15, as said below
Outputs:
- normalized_power: float32 [32, 64, 4096], P('dm', None, 'chan')
Inputs may be any that keep to these rules, and one draw needn't show every extreme that they name: `stretch_owner`: the owners of the 4 stretches are distinct slots. `tap_blocks`: never falls from one trial to the next.
All inputs are finite; a program needn't handle non-finite values.
Results may differ from a plain program's by a relative error of at most 0.0003.
Values may be sent and summed in bfloat16 or wider, within the bound.
A program may use at most 128 MiB of HBM per device.

v0:
```python
import jax
import jax.numpy as jnp
from jax import lax
from jax.sharding import PartitionSpec as P

CHANS = 4096
BLOCK = 64
STRETCHES = 4
DOWN = 16


epsilon = 1e-06


def spread(value, axis, source):
    kept = jnp.where(lax.axis_index(axis) == source, value, 0).astype(value.dtype)
    return lax.psum(kept, axis)


def masked_taps(tap_slab, tap_widths):
    tap_count = tap_slab.shape[2] // 2
    live = jnp.arange(tap_count, dtype=jnp.int32)[None, :] < tap_widths[:, None]
    live_both = jnp.concatenate([live, live], axis=1).astype(tap_slab.dtype)
    return tap_slab * live_both[:, None, :]


def build_kernel(tap_slab):
    tap_count = tap_slab.shape[2] // 2
    real_taps = tap_slab[:, :, :tap_count][:, :, ::-1]
    imag_taps = tap_slab[:, :, tap_count:][:, :, ::-1]
    from_real = jnp.stack([real_taps, imag_taps], axis=-1)
    from_imag = jnp.stack([-imag_taps, real_taps], axis=-1)
    stacked = jnp.stack([from_real, from_imag], axis=2)
    return stacked.transpose(3, 1, 2, 0, 4).reshape(tap_count, 1, -1)


def make_signal(previous, arrived):
    extended = jnp.concatenate([previous, arrived], axis=0)
    groups = extended.shape[2]
    return extended.transpose(0, 2, 1).reshape(1, -1, groups * 2)


def conv_power(signal, kernel, span_taps):
    tap_count = kernel.shape[0]
    features = signal.shape[2]
    channel_count = features // 2
    offset = 1 + tap_count - span_taps
    filtered = lax.conv_general_dilated(
        signal[:, offset:, :],
        kernel,
        (1,),
        "VALID",
        dimension_numbers=("NWC", "WIO", "NWC"),
        feature_group_count=features,
        preferred_element_type=jnp.float32,
    )
    length = filtered.shape[1]
    filtered = filtered.reshape(length, channel_count, 2, -1, 2)
    combined = jnp.sum(filtered, axis=2)
    energy = jnp.sum(combined * combined, axis=3)
    return jnp.sum(energy.reshape(length // DOWN, DOWN, channel_count, -1), axis=1) / DOWN


def respond(signal, kernel):
    tap_count = kernel.shape[0]
    return conv_power(signal, kernel, tap_count)


def fetch_stretch(held_stretch, owner):
    return spread(held_stretch, "dm", owner)


def body(phased, filters, tap_blocks, stretch_owner):
    held_stretch = phased[0]
    trials_dev = filters.shape[0]
    chan_count = filters.shape[1]
    tap_count = filters.shape[2] // 2
    my_index = lax.axis_index("dm")
    widths = tap_blocks * BLOCK
    my_widths = lax.dynamic_slice_in_dim(widths, my_index * trials_dev, trials_dev)
    kernel = build_kernel(masked_taps(filters, my_widths))
    previous = jnp.zeros((tap_count, 2, chan_count), held_stretch.dtype)
    pieces = []
    for index in range(STRETCHES):
        arrived = fetch_stretch(held_stretch, stretch_owner[index])
        signal = make_signal(previous, arrived)
        pieces.append(respond(signal, kernel))
        previous = arrived
    detected = jnp.concatenate(pieces, axis=0).transpose(2, 0, 1)
    band_total = lax.psum(jnp.sum(detected, axis=2), "chan")
    band_mean = band_total / CHANS
    return detected / (band_mean[:, :, None] + epsilon)


def solution(mesh):
    in_specs = (P("dm", None, None, "chan"), P("dm", "chan", None), P(), P())
    out_specs = P("dm", None, "chan")
    return jax.shard_map(body, mesh=mesh, in_specs=in_specs, out_specs=out_specs, check_vma=False)
```

profile of v0, /device:TPU:0, one launch (start us, length us, event | category | flops | bytes accessed | tf_op | source)
XLA Modules:
  0.0 2757.5 jit_solution(8658398344542953788)
XLA Ops:
  10.5 8.2 fusion
  24.3 27.4 rev.7
  51.7 31.9 %rev.6 = bf16[2,2048,256]{2,1,0:T(8,128)(2,1)} reverse(bf16[2,2048,256]{2,1,0:T(8,128)(2,1)} %get-tuple-element.10), dimensions={2} | reverse | bytes 4194304 | tf_op jit(solution)/shard_map/rev | solution.py:29
  88.8 7.5 maximum_bitcast_fusion
  96.3 16.5 copy.75
  112.8 13.2 reshape.101
  126.0 36.9 %copy.77 = bf16[256,1,4096,4]{2,1,3,0:T(2,128)(2,1)} copy(bf16[256,1,4096,4]{0,2,3,1:T(8,128)(2,1)} %reshape.101) | data formatting | bytes 16777216 | tf_op jit(solution)/shard_map/reshape
  162.9 118.2 %all-reduce.4.cloned.1.call-done = (bf16[256,2,2048]{2,1,0:T(2,128)(2,1)}, bf16[256,2,2048]{2,1,0:T(2,128)(2,1)}, bf16[256,2,2048]{2,1,0:T(2,128)(2,1)}, bf16[256,2,2048]{2,1,0:T(2,128)(2,1)}) async-done(((bf16[256,2,2048]{2,1,0:T(2,128)(2,1)}, bf16[256,2,2048]{2,1,0:T(2,128)(2,1)}, bf16[256,2,2048]{2,1,0:T(2,128)(2,1)}, bf16[256,2,2048]{2,1,0:T(2,128)(2,1)}), (bf16[256,2,2048]{2,1,0:T(2,128)(2,1)}, ...) | async-done | bytes 8388624 | tf_op jit(solution)/shard_map/psum | solution.py:17
  281.1 21.9 pad_bitcast_fusion
  303.0 16.0 copy.80
  318.9 7.2 reshape.104
  326.1 6.5 slice_bitcast_fusion.2
  332.7 18.8 copy.82
  351.4 441.5 %fusion.9 = f32[1,256,4096,4]{2,0,3,1:T(1,128)} fusion(bf16[1,511,4096,1]{2,0,3,1:T(2,128)(2,1)} %copy.82, bf16[256,1,4096,4]{2,1,3,0:T(2,128)(2,1)} %copy.77), kind=kOutput, calls=%fused_computation.43 | convolution fusion | flops 2147483648 | bytes 29351936 | tf_op jit(solution)/shard_map/convolution.1
  793.0 37.3 %copy.84 = f32[1,256,4096,4]{1,2,3,0:T(8,128)} copy(f32[1,256,4096,4]{2,0,3,1:T(1,128)} %fusion.9) | data formatting | bytes 33554432 | tf_op jit(solution)/shard_map/convolution.1
  830.2 20.0 reshape.106
  850.3 48.0 %reduce_sum.120 = f32[256,2048,2,2]{0,1,3,2:T(8,128)} reduce(f32[256,2048,2,2,2]{0,2,1,4,3:T(2,128)} %reshape.106, f32[]{:T(128)} %constant.34.clone.1), dimensions={2}, to_apply=%region_5.6 | reduce | flops 2097152 | bytes 25165828 | tf_op jit(solution)/shard_map/reduce_sum | solution.py:59
  898.3 6.5 multiply_reduce_fusion.2
  904.8 5.4 copy.85
  913.9 15.9 copy.73
  929.8 7.6 reshape.99
  937.4 6.5 slice_bitcast_fusion.3
  943.9 18.8 copy.76
  962.7 441.3 %fusion.8 = f32[1,256,4096,4]{2,0,3,1:T(1,128)} fusion(bf16[1,511,4096,1]{2,0,3,1:T(2,128)(2,1)} %copy.76, bf16[256,1,4096,4]{2,1,3,0:T(2,128)(2,1)} %copy.77), kind=kOutput, calls=%fused_computation.42 | convolution fusion | flops 2147483648 | bytes 29351936 | tf_op jit(solution)/shard_map/convolution
  1404.0 37.3 %copy.78 = f32[1,256,4096,4]{1,2,3,0:T(8,128)} copy(f32[1,256,4096,4]{2,0,3,1:T(1,128)} %fusion.8) | data formatting | bytes 33554432 | tf_op jit(solution)/shard_map/convolution
  1441.3 20.0 reshape.102
  1461.3 48.0 %reduce_sum.117 = f32[256,2048,2,2]{0,1,3,2:T(8,128)} reduce(f32[256,2048,2,2,2]{0,2,1,4,3:T(2,128)} %reshape.102, f32[]{:T(128)} %constant.34.clone.1), dimensions={2}, to_apply=%region_1.2 | reduce | flops 2097152 | bytes 25165828 | tf_op jit(solution)/shard_map/reduce_sum | solution.py:59
  1509.4 6.5 multiply_reduce_fusion.3
  1515.9 5.6 copy.79
  1525.1 15.9 copy.86
  1541.1 7.2 reshape.108
  1548.3 6.5 slice_bitcast_fusion.1
  1554.8 18.8 copy.88
  1573.6 441.3 %fusion.10 = f32[1,256,4096,4]{2,0,3,1:T(1,128)} fusion(bf16[1,511,4096,1]{2,0,3,1:T(2,128)(2,1)} %copy.88, bf16[256,1,4096,4]{2,1,3,0:T(2,128)(2,1)} %copy.77), kind=kOutput, calls=%fused_computation.44 | convolution fusion | flops 2147483648 | bytes 29351936 | tf_op jit(solution)/shard_map/convolution.2
  2014.9 37.3 %copy.90 = f32[1,256,4096,4]{1,2,3,0:T(8,128)} copy(f32[1,256,4096,4]{2,0,3,1:T(1,128)} %fusion.10) | data formatting | bytes 33554432 | tf_op jit(solution)/shard_map/convolution.2
  2052.1 20.0 reshape.110
  2072.2 48.3 %reduce_sum.123 = f32[256,2048,2,2]{0,1,3,2:T(8,128)} reduce(f32[256,2048,2,2,2]{0,2,1,4,3:T(2,128)} %reshape.110, f32[]{:T(128)} %constant.34.clone.1), dimensions={2}, to_apply=%region_9.10 | reduce | flops 2097152 | bytes 25165828 | tf_op jit(solution)/shard_map/reduce_sum | solution.py:59
  2120.4 6.5 multiply_reduce_fusion.1
  2126.9 5.4 copy.91
  2136.0 15.9 copy.92
  2152.0 7.2 reshape.112
  2159.2 6.5 slice_bitcast_fusion
  2165.7 18.8 copy.94
  2184.5 441.3 %fusion.11 = f32[1,256,4096,4]{2,0,3,1:T(1,128)} fusion(bf16[1,511,4096,1]{2,0,3,1:T(2,128)(2,1)} %copy.94, bf16[256,1,4096,4]{2,1,3,0:T(2,128)(2,1)} %copy.77), kind=kOutput, calls=%fused_computation.45 | convolution fusion | flops 2147483648 | bytes 29351936 | tf_op jit(solution)/shard_map/convolution.3
  2625.8 37.1 %copy.96 = f32[1,256,4096,4]{1,2,3,0:T(8,128)} copy(f32[1,256,4096,4]{2,0,3,1:T(1,128)} %fusion.11) | data formatting | bytes 33554432 | tf_op jit(solution)/shard_map/convolution.3
  2662.9 20.0 reshape.114
  2683.0 48.3 %reduce_sum.126 = f32[256,2048,2,2]{0,1,3,2:T(8,128)} reduce(f32[256,2048,2,2,2]{0,2,1,4,3:T(2,128)} %reshape.114, f32[]{:T(128)} %constant.34.clone.1), dimensions={2}, to_apply=%region_13.14 | reduce | flops 2097152 | bytes 25165828 | tf_op jit(solution)/shard_map/reduce_sum | solution.py:59
  2731.3 6.6 multiply_reduce_fusion
  (32 shorter events, 35.5 us)
Async XLA Ops:
  6.5 274.5 %all-reduce.4.cloned.1.call-start = ((), (), s32[]{:S(2)}) async-start(), calls=%async_computation | async-start | bytes 16777216 | tf_op jit(solution)/shard_map/psum | solution.py:17
  18.7 0.7 copy-start.4
  83.6 1.6 copy-start
  2743.2 3.1 copy-start.1
  2743.2 3.1 copy-start.2
  2743.2 3.2 copy-start.3
Sparse Core Ops, SparseCore 0:
  18.9 262.1 all-reduce.3
where the time goes:
time: 2780 us; the launch traced here: 2760 us
  matrix products  1770 us (64%)
  local copies, waits for them, and re-layouts  577 us (21%)
  other arithmetic  278 us (10%)
  waiting for transfers between devices  118 us (4%)
    another operation x4, matrix products  1770 us
    another operation x12, local copies, waits for them, and re-layouts  250 us
    reduce_sum x4, other arithmetic, conv_power(): combined = jnp.sum(filtered, axis=2)  193 us
    psum x1, waiting for transfers between devices, spread(): return lax.psum(kept, axis)  118 us
    reshape x4, local copies, waits for them, and re-layouts, conv_power(): filtered = filtered.reshape(length, channel_count, 2, -1, 2)  80.2 us
    transpose x4, local copies, waits for them, and re-layouts, make_signal(): return extended.transpose(0, 2, 1).reshape(1, -1, groups * 2)  63.8 us
  transfers between devices with their start and end apart: 1, of which 1 were waited for; matrix products, arithmetic and copies ran while one was open for 5% of the time, Pallas kernels for 0%

commit v1 on v0

v1 whole, which is shorter than its diff:
```python
import functools

import jax
import jax.numpy as jnp
import ml_dtypes
import numpy as np
from jax import lax
from jax.experimental import pallas as pl
from jax.experimental.pallas import tpu as pltpu
from jax.sharding import PartitionSpec as P

CHANS = 4096
TAPS = 256
BLOCK = 64
SAMPLES = 256
STRETCHES = 4
DOWN = 16
SPAN = 2 * BLOCK
NBLOCKS = TAPS // BLOCK
WIDE = 256
ROWS = 16

epsilon = 1e-06

LAST_BITS = ((2, 1, 0), (2, 0, 1), (0, 1, 2), (1, 0, 2))


def split_high_low(matrix):
    high = matrix.astype(ml_dtypes.bfloat16)
    low = (matrix - high.astype(np.float64)).astype(ml_dtypes.bfloat16)
    return high, low


def signal_transform():
    angle = 2 * np.pi * np.outer(np.arange(SPAN), np.arange(SPAN)) / SPAN
    out = np.zeros((2, SPAN, SPAN, 2))
    out[0, :, :, 0] = np.cos(angle)
    out[0, :, :, 1] = np.sin(angle)
    out[1, :, :, 0] = -np.sin(angle)
    out[1, :, :, 1] = np.cos(angle)
    return np.concatenate(split_high_low(out.reshape(2 * SPAN, 2 * SPAN)), axis=0)


def filter_transform():
    angle = 2 * np.pi * np.outer(np.arange(SPAN), np.arange(BLOCK)) / SPAN
    out = np.zeros((NBLOCKS, 2, SPAN, 2, NBLOCKS, BLOCK))
    for block in range(NBLOCKS):
        out[block, 0, :, 0, block] = np.cos(angle)
        out[block, 0, :, 1, block] = np.sin(angle)
        out[block, 1, :, 0, block] = -np.sin(angle)
        out[block, 1, :, 1, block] = np.cos(angle)
    out = out.reshape(NBLOCKS, 2 * SPAN, 2 * TAPS)
    return np.concatenate(split_high_low(out), axis=1)


def inverse_transform():
    groups = BLOCK // DOWN
    times = (np.arange(groups)[None, :] * DOWN + np.arange(DOWN)[:, None]).reshape(-1)
    angle = 2 * np.pi * np.outer(BLOCK + times, np.arange(SPAN)) / SPAN
    real = np.concatenate([np.cos(angle), -np.sin(angle)], axis=1)
    imag = np.concatenate([np.sin(angle), np.cos(angle)], axis=1)
    out = np.concatenate([real, imag], axis=0) / SPAN
    return np.concatenate(split_high_low(out), axis=0)


def dot(a, b):
    return jnp.dot(a, b, preferred_element_type=jnp.float32)


def kernel(trials, chunks, place_ref, live_ref, s0, s1, s2, s3, filters_ref, d_ref, g_ref, e_ref, out_ref, line, spec, resp, zhigh, zlow):
    rows = 2 * SAMPLES // chunks
    line[0:SPAN, :] = jnp.zeros((SPAN, WIDE), line.dtype)
    for k, source in enumerate((s0, s1, s2, s3)):
        for i in range(chunks):
            first = SPAN + k * 2 * SAMPLES + i * rows
            line[first:first + rows, :] = source[place_ref[k, i]]

    for p in range(NBLOCKS - 1):
        spec[p] = jnp.zeros((2 * SPAN, WIDE), jnp.float32)
    steps = STRETCHES * SAMPLES // BLOCK

    def forward(b, carry):
        window = line[pl.ds(pl.multiple_of(b * SPAN, SPAN), 2 * SPAN), :]
        spec[b + NBLOCKS - 1] = dot(d_ref[:2 * SPAN], window) + dot(d_ref[2 * SPAN:], window)
        return carry

    lax.fori_loop(0, steps, forward, 0)

    for t in range(trials):
        taps = filters_ref[t]
        for p in range(NBLOCKS):
            both = lax.dot_general(g_ref[p], taps, (((1,), (1,)), ((), ())), preferred_element_type=jnp.float32)
            live = (p < live_ref[t]).astype(jnp.float32)
            resp[t, p] = (both[:2 * SPAN] + both[2 * SPAN:]) * live

    groups = BLOCK // DOWN

    def outputs(pair, carry):
        powers = [[] for _ in range(trials)]
        for half in range(2):
            b = pair * 2 + half
            for c in range(SPAN // ROWS):
                re = slice(c * ROWS, (c + 1) * ROWS)
                im = slice(SPAN + c * ROWS, SPAN + (c + 1) * ROWS)
                sums = [None] * trials
                for p in range(NBLOCKS):
                    xr = spec[b + NBLOCKS - 1 - p, re, :]
                    xi = spec[b + NBLOCKS - 1 - p, im, :]
                    for t in range(trials):
                        hr = resp[t, p, re, :]
                        hi = resp[t, p, im, :]
                        zr = xr * hr - xi * hi
                        zi = xr * hi + xi * hr
                        sums[t] = (zr, zi) if p == 0 else (sums[t][0] + zr, sums[t][1] + zi)
                for t in range(trials):
                    for part, z in zip((re, im), sums[t]):
                        high = z.astype(jnp.bfloat16)
                        zhigh[half, t, part, :] = high
                        zlow[half, t, part, :] = (z - high.astype(jnp.float32)).astype(jnp.bfloat16)
            for t in range(trials):
                both = dot(e_ref[...], zhigh[half, t])
                y = both[:SPAN] + both[SPAN:] + dot(e_ref[:SPAN], zlow[half, t])
                energy = jnp.sum((y * y).reshape(SPAN // 8, 8, WIDE), axis=0)
                powers[t].append(energy[:groups] + energy[groups:])
        for t in range(trials):
            rows_out = pl.ds(pl.multiple_of(pair * 2 * groups, 2 * groups), 2 * groups)
            out_ref[t, rows_out, :] = jnp.concatenate(powers[t], axis=0) * (1.0 / DOWN)
        return carry

    lax.fori_loop(0, steps // 2, outputs, 0)


def detect(signals, filters, place, live):
    trials, chans, _ = filters.shape
    chunks, rows, _ = signals[0].shape
    times = STRETCHES * SAMPLES // DOWN
    steps = STRETCHES * SAMPLES // BLOCK
    d, g, e = signal_transform(), filter_transform(), inverse_transform()
    smem = pl.BlockSpec(memory_space=pltpu.SMEM)
    return pl.pallas_call(
        functools.partial(kernel, trials, chunks),
        grid=(chans // WIDE,),
        out_shape=jax.ShapeDtypeStruct((trials, times, chans), jnp.float32),
        in_specs=[smem, smem]
        + [pl.BlockSpec((chunks, rows, WIDE), lambda c: (0, 0, c))] * STRETCHES
        + [
            pl.BlockSpec((trials, WIDE, 2 * TAPS), lambda c: (0, c, 0)),
            pl.BlockSpec(d.shape, lambda c: (0, 0)),
            pl.BlockSpec(g.shape, lambda c: (0, 0, 0)),
            pl.BlockSpec(e.shape, lambda c: (0, 0)),
        ],
        out_specs=pl.BlockSpec((trials, times, WIDE), lambda c: (0, 0, c)),
        scratch_shapes=[
            pltpu.VMEM((SPAN + STRETCHES * 2 * SAMPLES, WIDE), jnp.bfloat16),
            pltpu.VMEM((steps + NBLOCKS - 1, 2 * SPAN, WIDE), jnp.float32),
            pltpu.VMEM((trials, NBLOCKS, 2 * SPAN, WIDE), jnp.float32),
            pltpu.VMEM((2, trials, 2 * SPAN, WIDE), jnp.bfloat16),
            pltpu.VMEM((2, trials, 2 * SPAN, WIDE), jnp.bfloat16),
        ],
        compiler_params=pltpu.CompilerParams(vmem_limit_bytes=40 * 1024 * 1024),
        cost_estimate=pl.CostEstimate(flops=30_000_000_000, bytes_accessed=16_000_000, transcendentals=0),
    )(place, live, *signals, filters, jnp.asarray(d), jnp.asarray(g), jnp.asarray(e))


def swap(value, axis, size, bit):
    return lax.ppermute(value, axis, [(i, i ^ (1 << bit)) for i in range(size)])


def body(dm, chan, phased, filters, tap_blocks, stretch_owner):
    trials, chans, _ = filters.shape
    me = lax.axis_index("dm")
    rows = 2 * SAMPLES // dm
    bits = dm.bit_length() - 1

    held = phased.reshape(dm, rows, chans)
    slots = lax.all_to_all(held, "dm", 0, 0, tiled=True)
    owned = [lax.dynamic_slice_in_dim(slots, stretch_owner[k], 1, 0) for k in range(STRETCHES)]
    orders = []
    for k in range(STRETCHES):
        low = [bit for bit in LAST_BITS[k] if bit < bits]
        orders.append(list(range(bits - 1, 2, -1)) + low)
    for s in range(bits):
        owned = [jnp.concatenate([a, swap(a, "dm", dm, orders[k][s])], axis=0) for k, a in enumerate(owned)]

    away = jnp.arange(dm, dtype=jnp.int32) ^ me
    place = jnp.stack([sum(((away >> orders[k][s]) & 1) << s for s in range(bits)) for k in range(STRETCHES)])
    live = lax.dynamic_slice_in_dim(tap_blocks, me * trials, trials)

    detected = detect(owned, filters, place, live)
    band = jnp.sum(detected, axis=2)
    for bit in range(chan.bit_length() - 1):
        band = band + swap(band, "chan", chan, bit)
    return detected / (band[:, :, None] / CHANS + epsilon)


def solution(mesh):
    in_specs = (P("dm", None, None, "chan"), P("dm", "chan", None), P(), P())
    out_specs = P("dm", None, "chan")
    run = functools.partial(body, mesh.shape["dm"], mesh.shape["chan"])
    return jax.shard_map(run, mesh=mesh, in_specs=in_specs, out_specs=out_specs, check_vma=False)
```

time: 2780 us -> 283 us (0.10)
  matrix products: 1770 us -> 0 us
  local copies, waits for them, and re-layouts: 577 us -> 8.71 us
  other arithmetic: 278 us -> 2.05 us
  Pallas kernels: 0 us -> 115 us
    another operation x4 -> x0, matrix products: 1770 us -> none
    another operation x12 -> x0, local copies, waits for them, and re-layouts: 250 us -> none
    reduce_sum x13 -> x1, other arithmetic: 233 us -> 0.14 us  [body(): band = jnp.sum(detected, axis=2)]
    reshape x10 -> x1, local copies, waits for them, and re-layouts: 159 us -> 4.1 us  [body(): held = phased.reshape(dm, rows, chans)]
    psum x1 -> x0, waiting for transfers between devices: 118 us -> none  [spread(): return lax.psum(kept, axis)]
    pallas_call x0 -> x1, Pallas kernels: none -> 115 us  [detect(): pl.pallas_call(functools.partial(kernel, trials, chunks), grid=(chans //...]
    ppermute x0 -> x17, waiting for transfers between devices: none -> 86.9 us  [swap(): return lax.ppermute(value, axis, [(i, i ^ 1 << bit) for i in range(size)])]
    transpose x5 -> x0, local copies, waits for them, and re-layouts: 80.3 us -> none  [the longest x4 63.8 us: make_signal(): return extended.transpose(0, 2, 1).reshape(1, -1, groups * 2)]
  transfers between devices with their start and end apart: 1 -> 18, of which waited for: 1 -> 14; matrix products, arithmetic and copies ran while one was open for 5% -> 1% of each run, Pallas kernels for 0% -> 0%
where the time goes in v1:
time: 283 us; the launch traced here: 282 us
  waiting for transfers between devices  122 us (43%)
  Pallas kernels  115 us (41%)
  starting transfers between devices  26.9 us (10%)
  local copies, waits for them, and re-layouts  8.71 us (3%)
  between operations  7.88 us (3%)
    pallas_call x1, Pallas kernels, detect(): pl.pallas_call(functools.partial(kernel, trials, chunks), grid=(chans //...  115 us
    ppermute x17, waiting for transfers between devices, swap(): return lax.ppermute(value, axis, [(i, i ^ 1 << bit) for i in range(size)])  86.9 us
    all_to_all x1, waiting for transfers between devices, body(): slots = lax.all_to_all(held, 'dm', 0, 0, tiled=True)  34.9 us
    ppermute x17, starting transfers between devices, swap(): return lax.ppermute(value, axis, [(i, i ^ 1 << bit) for i in range(size)])  18.4 us
    all_to_all x1, starting transfers between devices, body(): slots = lax.all_to_all(held, 'dm', 0, 0, tiled=True)  8.5 us
  transfers between devices with their start and end apart: 18, of which 14 were waited for; matrix products, arithmetic and copies ran while one was open for 1% of the time, Pallas kernels for 0%

profile of v1, /device:TPU:0, one launch (start us, length us, event | category | flops | bytes accessed | tf_op | source)
XLA Modules:
  0.0 282.2 jit_solution(13519771483292063438)
XLA Ops:
  0.0 4.1 %reshape.100 = bf16[16,32,2048]{2,1,0:T(8,128)(2,1)} reshape(bf16[1,256,2,2048]{3,2,1,0:T(2,128)(2,1)} %param.7) | data formatting | bytes 4194304 | tf_op jit(solution)/shard_map/reshape | solution.py:175
  4.1 8.5 %all-to-all-start = ((bf16[16,32,2048]{2,1,0:T(8,128)(2,1)}), bf16[16,32,2048]{2,1,0:T(8,128)(2,1)}, u32[]{:S(2)}, u32[]{:S(2)}) async-start(bf16[16,32,2048]{2,1,0:T(8,128)(2,1)} %reshape.100), calls=%async_computation | async-start | bytes 4194304 | tf_op jit(solution)/shard_map/all_to_all | solution.py:176
  12.6 0.7 fusion
  20.9 34.9 %all-to-all-done = bf16[16,32,2048]{2,1,0:T(8,128)(2,1)} async-done(((bf16[16,32,2048]{2,1,0:T(8,128)(2,1)}), bf16[16,32,2048]{2,1,0:T(8,128)(2,1)}, u32[]{:S(2)}, u32[]{:S(2)}) %all-to-all-start) | async-done | bytes 2097184 | tf_op jit(solution)/shard_map/all_to_all | solution.py:176
  55.7 1.9 constant_dynamic-update-slice_fusion.19
  57.6 7.8 %collective-permute-start = (bf16[1,32,2048]{2,1,0:T(8,128)(2,1)S(1)}, bf16[1,32,2048]{2,1,0:T(8,128)(2,1)S(1)}, u32[]{:S(2)}, u32[]{:S(2)}) collective-permute-start(bf16[1,32,2048]{2,1,0:T(8,128)(2,1)S(1)} %get-tuple-element.18), channel_id=1, source_target_pairs={{0,16},{2,18},{4,20},{6,22},{8,24},{10,26},{12,28},{14,30},{16,0},... | collective-permute-start | bytes 393224 | tf_op jit(solution)/shard_map/ppermute | solution.py:166
  65.4 0.1 dynamic_slice.15.live_ref
  65.5 0.1 collective-permute-start.4
  65.6 2.9 %collective-permute-start.8 = (bf16[1,32,2048]{2,1,0:T(8,128)(2,1)S(1)}, bf16[1,32,2048]{2,1,0:T(8,128)(2,1)S(1)}, u32[]{:S(2)}, u32[]{:S(2)}) collective-permute-start(bf16[1,32,2048]{2,1,0:T(8,128)(2,1)S(1)} %get-tuple-element.14), channel_id=1, source_target_pairs={{0,16},{2,18},{4,20},{6,22},{8,24},{10,26},{12,28},{14,30},{16,0},... | collective-permute-start | bytes 393224 | tf_op jit(solution)/shard_map/ppermute | solution.py:166
  68.5 0.1 collective-permute-start.12
  68.6 10.2 %collective-permute-done = bf16[1,32,2048]{2,1,0:T(8,128)(2,1)S(1)} collective-permute-done((bf16[1,32,2048]{2,1,0:T(8,128)(2,1)S(1)}, bf16[1,32,2048]{2,1,0:T(8,128)(2,1)S(1)}, u32[]{:S(2)}, u32[]{:S(2)}) %collective-permute-start) | collective-permute-done | bytes 131104 | tf_op jit(solution)/shard_map/ppermute | solution.py:166
  78.9 0.7 collective-permute-start.1
  79.6 2.1 collective-permute-done.4
  81.7 0.7 collective-permute-start.5
  82.4 2.2 collective-permute-done.8
  84.6 1.3 collective-permute-start.9
  85.9 1.3 collective-permute-done.12
  87.2 0.4 collective-permute-start.13
  87.6 0.7 constant_dynamic-update-slice_fusion.3
  88.3 0.6 constant_dynamic-update-slice_fusion.8
  89.0 3.8 %collective-permute-done.1 = bf16[2,32,2048]{2,1,0:T(8,128)(2,1)S(1)} collective-permute-done((bf16[2,32,2048]{2,1,0:T(8,128)(2,1)S(1)}, bf16[2,32,2048]{2,1,0:T(8,128)(2,1)S(1)}, u32[]{:S(2)}, u32[]{:S(2)}) %collective-permute-start.1) | collective-permute-done | bytes 262176 | tf_op jit(solution)/shard_map/ppermute | solution.py:166
  92.9 0.4 collective-permute-start.2
  93.3 5.1 %collective-permute-done.5 = bf16[2,32,2048]{2,1,0:T(8,128)(2,1)S(1)} collective-permute-done((bf16[2,32,2048]{2,1,0:T(8,128)(2,1)S(1)}, bf16[2,32,2048]{2,1,0:T(8,128)(2,1)S(1)}, u32[]{:S(2)}, u32[]{:S(2)}) %collective-permute-start.5) | collective-permute-done | bytes 262176 | tf_op jit(solution)/shard_map/ppermute | solution.py:166
  98.4 0.9 collective-permute-start.6
  99.3 0.4 collective-permute-start.10
  99.8 1.3 collective-permute-start.14
  101.2 6.6 %collective-permute-done.2 = bf16[4,32,2048]{2,1,0:T(8,128)(2,1)S(1)} collective-permute-done((bf16[4,32,2048]{2,1,0:T(8,128)(2,1)S(1)}, bf16[4,32,2048]{2,1,0:T(8,128)(2,1)S(1)}, u32[]{:S(2)}, u32[]{:S(2)}) %collective-permute-start.2) | collective-permute-done | bytes 524320 | tf_op jit(solution)/shard_map/ppermute | solution.py:166
  107.7 0.1 pad_maximum_fusion
  107.8 0.9 collective-permute-start.3
  108.7 4.5 %collective-permute-done.6 = bf16[4,32,2048]{2,1,0:T(8,128)(2,1)S(1)} collective-permute-done((bf16[4,32,2048]{2,1,0:T(8,128)(2,1)S(1)}, bf16[4,32,2048]{2,1,0:T(8,128)(2,1)S(1)}, u32[]{:S(2)}, u32[]{:S(2)}) %collective-permute-start.6) | collective-permute-done | bytes 524320 | tf_op jit(solution)/shard_map/ppermute | solution.py:166
  113.2 0.1 pad_maximum_fusion.1
  113.3 0.4 collective-permute-start.7
  113.7 5.2 %collective-permute-done.10 = bf16[4,32,2048]{2,1,0:T(8,128)(2,1)S(1)} collective-permute-done((bf16[4,32,2048]{2,1,0:T(8,128)(2,1)S(1)}, bf16[4,32,2048]{2,1,0:T(8,128)(2,1)S(1)}, u32[]{:S(2)}, u32[]{:S(2)}) %collective-permute-start.10) | collective-permute-done | bytes 524320 | tf_op jit(solution)/shard_map/ppermute | solution.py:166
  119.0 0.1 pad_maximum_fusion.2
  119.1 0.1 collective-permute-start.11
  119.2 5.3 %collective-permute-done.14 = bf16[4,32,2048]{2,1,0:T(8,128)(2,1)S(1)} collective-permute-done((bf16[4,32,2048]{2,1,0:T(8,128)(2,1)S(1)}, bf16[4,32,2048]{2,1,0:T(8,128)(2,1)S(1)}, u32[]{:S(2)}, u32[]{:S(2)}) %collective-permute-start.14) | collective-permute-done | bytes 524320 | tf_op jit(solution)/shard_map/ppermute | solution.py:166
  124.5 0.1 pad_maximum_fusion.3
  124.6 0.1 collective-permute-start.15
  124.8 21.1 %collective-permute-done.3 = bf16[8,32,2048]{2,1,0:T(8,128)(2,1)S(1)} collective-permute-done((bf16[8,32,2048]{2,1,0:T(8,128)(2,1)S(1)}, bf16[8,32,2048]{2,1,0:T(8,128)(2,1)S(1)}, u32[]{:S(2)}, u32[]{:S(2)}) %collective-permute-start.3) | collective-permute-done | bytes 1048608 | tf_op jit(solution)/shard_map/ppermute | solution.py:166
  146.0 0.1 constant_dynamic-update-slice_fusion.s0
  146.1 0.1 constant_dynamic-update-slice_fusion.5.s1
  146.3 0.1 constant_dynamic-update-slice_fusion.10.s2
  146.4 18.3 %collective-permute-done.15 = bf16[8,32,2048]{2,1,0:T(8,128)(2,1)S(1)} collective-permute-done((bf16[8,32,2048]{2,1,0:T(8,128)(2,1)S(1)}, bf16[8,32,2048]{2,1,0:T(8,128)(2,1)S(1)}, u32[]{:S(2)}, u32[]{:S(2)}) %collective-permute-start.15) | collective-permute-done | bytes 1048608 | tf_op jit(solution)/shard_map/ppermute | solution.py:166
  164.7 0.1 constant_dynamic-update-slice_fusion.15.s3
  164.8 115.0 %shard_map.73 = f32[2,64,2048]{2,1,0:T(8,128)S(1)} custom-call(s32[4,16]{1,0:T(4,128)S(1)} %pad_add_fusion.place_ref, s32[2]{0:T(128)S(1)} %dynamic_slice.15.live_ref, bf16[16,32,2048]{2,1,0:T(8,128)(2,1)S(1)} %constant_dynamic-update-slice_fusion.s0, bf16[16,32,2048]{2,1,0:T(8,128)(2,1)S(1)} %constant_dynamic-update-slice_fusion.5.s1, ...), custom_call_target="tpu_custom_call" | custom-call | flops 30000001024 | bytes 16000000 | tf_op jit(solution)/shard_map/pallas_call | solution.py:140
  279.8 0.1 reduce_sum.9
  280.0 1.1 collective-permute-done.16
  281.1 1.1 broadcast_divide_fusion
  (43 shorter events, 0.7 us)
Async XLA Ops:
  4.1 8.5 %copy-start.6 = (s32[4]{0:T(128)S(1)}, s32[4]{0:T(128)}, u32[]{:S(2)}) copy-start(s32[4]{0:T(128)} %param.10) | copy-start | bytes 52
  4.1 61.3 %copy-start.7 = (s32[32]{0:T(128)S(1)}, s32[32]{0:T(128)}, u32[]{:S(2)}) copy-start(s32[32]{0:T(128)} %param.9) | copy-start | bytes 388
  4.1 51.6 %all-to-all-start = ((bf16[16,32,2048]{2,1,0:T(8,128)(2,1)}), bf16[16,32,2048]{2,1,0:T(8,128)(2,1)}, u32[]{:S(2)}, u32[]{:S(2)}) async-start(bf16[16,32,2048]{2,1,0:T(8,128)(2,1)} %reshape.100), calls=%async_computation | async-start | bytes 4194304 | tf_op jit(solution)/shard_map/all_to_all | solution.py:176
  57.6 21.2 %collective-permute-start = (bf16[1,32,2048]{2,1,0:T(8,128)(2,1)S(1)}, bf16[1,32,2048]{2,1,0:T(8,128)(2,1)S(1)}, u32[]{:S(2)}, u32[]{:S(2)}) collective-permute-start(bf16[1,32,2048]{2,1,0:T(8,128)(2,1)S(1)} %get-tuple-element.18), channel_id=1, source_target_pairs={{0,16},{2,18},{4,20},{6,22},{8,24},{10,26},{12,28},{14,30},{16,0},... | collective-permute-start | bytes 393224 | tf_op jit(solution)/shard_map/ppermute | solution.py:166
  65.4 23.5 %copy-start = (bf16[16,32,2048]{2,1,0:T(8,128)(2,1)S(1)}, bf16[16,32,2048]{2,1,0:T(8,128)(2,1)}, u32[]{:S(2)}) copy-start(bf16[16,32,2048]{2,1,0:T(8,128)(2,1)} %get-tuple-element.13) | copy-start | bytes 6291460
  65.5 16.2 %collective-permute-start.4 = (bf16[1,32,2048]{2,1,0:T(8,128)(2,1)S(1)}, bf16[1,32,2048]{2,1,0:T(8,128)(2,1)S(1)}, u32[]{:S(2)}, u32[]{:S(2)}) collective-permute-start(bf16[1,32,2048]{2,1,0:T(8,128)(2,1)S(1)} %get-tuple-element.16), channel_id=1, source_target_pairs={{0,16},{2,18},{4,20},{6,22},{8,24},{10,26},{12,28},{14,30},{16,0},... | collective-permute-start | bytes 393224 | tf_op jit(solution)/shard_map/ppermute | solution.py:166
  65.6 19.0 %collective-permute-start.8 = (bf16[1,32,2048]{2,1,0:T(8,128)(2,1)S(1)}, bf16[1,32,2048]{2,1,0:T(8,128)(2,1)S(1)}, u32[]{:S(2)}, u32[]{:S(2)}) collective-permute-start(bf16[1,32,2048]{2,1,0:T(8,128)(2,1)S(1)} %get-tuple-element.14), channel_id=1, source_target_pairs={{0,16},{2,18},{4,20},{6,22},{8,24},{10,26},{12,28},{14,30},{16,0},... | collective-permute-start | bytes 393224 | tf_op jit(solution)/shard_map/ppermute | solution.py:166
  68.5 18.7 %collective-permute-start.12 = (bf16[1,32,2048]{2,1,0:T(8,128)(2,1)S(1)}, bf16[1,32,2048]{2,1,0:T(8,128)(2,1)S(1)}, u32[]{:S(2)}, u32[]{:S(2)}) collective-permute-start(bf16[1,32,2048]{2,1,0:T(8,128)(2,1)S(1)} %get-tuple-element.6), channel_id=1, source_target_pairs={{0,16},{2,18},{4,20},{6,22},{8,24},{10,26},{12,28},{14,30},{16,0},... | collective-permute-start | bytes 393224 | tf_op jit(solution)/shard_map/ppermute | solution.py:166
  78.9 13.9 %collective-permute-start.1 = (bf16[2,32,2048]{2,1,0:T(8,128)(2,1)S(1)}, bf16[2,32,2048]{2,1,0:T(8,128)(2,1)S(1)}, u32[]{:S(2)}, u32[]{:S(2)}) collective-permute-start(bf16[2,32,2048]{2,1,0:T(8,128)(2,1)S(1)} %pad_maximum_fusion.8), channel_id=1, source_target_pairs={{0,8},{2,10},{4,12},{6,14},{8,0},{10,2},{12,4},{14,6},{16,24},{18,... | collective-permute-start | bytes 786440 | tf_op jit(solution)/shard_map/ppermute | solution.py:166
  81.7 16.6 %collective-permute-start.5 = (bf16[2,32,2048]{2,1,0:T(8,128)(2,1)S(1)}, bf16[2,32,2048]{2,1,0:T(8,128)(2,1)S(1)}, u32[]{:S(2)}, u32[]{:S(2)}) collective-permute-start(bf16[2,32,2048]{2,1,0:T(8,128)(2,1)S(1)} %pad_maximum_fusion.9), channel_id=1, source_target_pairs={{0,8},{2,10},{4,12},{6,14},{8,0},{10,2},{12,4},{14,6},{16,24},{18,... | collective-permute-start | bytes 786440 | tf_op jit(solution)/shard_map/ppermute | solution.py:166
  84.6 14.7 %collective-permute-start.9 = (bf16[2,32,2048]{2,1,0:T(8,128)(2,1)S(1)}, bf16[2,32,2048]{2,1,0:T(8,128)(2,1)S(1)}, u32[]{:S(2)}, u32[]{:S(2)}) collective-permute-start(bf16[2,32,2048]{2,1,0:T(8,128)(2,1)S(1)} %pad_maximum_fusion.10), channel_id=1, source_target_pairs={{0,2},{2,0},{4,6},{6,4},{8,10},{10,8},{12,14},{14,12},{16,18},{18,... | collective-permute-start | bytes 786440 | tf_op jit(solution)/shard_map/ppermute | solution.py:166
  87.2 12.5 %collective-permute-start.13 = (bf16[2,32,2048]{2,1,0:T(8,128)(2,1)S(1)}, bf16[2,32,2048]{2,1,0:T(8,128)(2,1)S(1)}, u32[]{:S(2)}, u32[]{:S(2)}) collective-permute-start(bf16[2,32,2048]{2,1,0:T(8,128)(2,1)S(1)} %pad_maximum_fusion.11), channel_id=1, source_target_pairs={{0,4},{2,6},{4,0},{6,2},{8,12},{10,14},{12,8},{14,10},{16,20},{18,... | collective-permute-start | bytes 786440 | tf_op jit(solution)/shard_map/ppermute | solution.py:166
  89.0 12.1 %copy-start.2 = (bf16[16,32,2048]{2,1,0:T(8,128)(2,1)S(1)}, bf16[16,32,2048]{2,1,0:T(8,128)(2,1)}, u32[]{:S(2)}) copy-start(bf16[16,32,2048]{2,1,0:T(8,128)(2,1)} %constant_dynamic-update-slice_fusion.3) | copy-start | bytes 6291460
  92.9 8.2 %copy-start.1 = (bf16[16,32,2048]{2,1,0:T(8,128)(2,1)S(1)}, bf16[16,32,2048]{2,1,0:T(8,128)(2,1)}, u32[]{:S(2)}) copy-start(bf16[16,32,2048]{2,1,0:T(8,128)(2,1)} %constant_dynamic-update-slice_fusion.8) | copy-start | bytes 6291460
  92.9 14.9 %collective-permute-start.2 = (bf16[4,32,2048]{2,1,0:T(8,128)(2,1)S(1)}, bf16[4,32,2048]{2,1,0:T(8,128)(2,1)S(1)}, u32[]{:S(2)}, u32[]{:S(2)}) collective-permute-start(bf16[4,32,2048]{2,1,0:T(8,128)(2,1)S(1)} %pad_maximum_fusion.4), channel_id=1, source_target_pairs={{0,4},{2,6},{4,0},{6,2},{8,12},{10,14},{12,8},{14,10},{16,20},{18,... | collective-permute-start | bytes 1572872 | tf_op jit(solution)/shard_map/ppermute | solution.py:166
  98.4 14.8 %collective-permute-start.6 = (bf16[4,32,2048]{2,1,0:T(8,128)(2,1)S(1)}, bf16[4,32,2048]{2,1,0:T(8,128)(2,1)S(1)}, u32[]{:S(2)}, u32[]{:S(2)}) collective-permute-start(bf16[4,32,2048]{2,1,0:T(8,128)(2,1)S(1)} %pad_maximum_fusion.5), channel_id=1, source_target_pairs={{0,2},{2,0},{4,6},{6,4},{8,10},{10,8},{12,14},{14,12},{16,18},{18,... | collective-permute-start | bytes 1572872 | tf_op jit(solution)/shard_map/ppermute | solution.py:166
  99.3 19.7 %collective-permute-start.10 = (bf16[4,32,2048]{2,1,0:T(8,128)(2,1)S(1)}, bf16[4,32,2048]{2,1,0:T(8,128)(2,1)S(1)}, u32[]{:S(2)}, u32[]{:S(2)}) collective-permute-start(bf16[4,32,2048]{2,1,0:T(8,128)(2,1)S(1)} %pad_maximum_fusion.6), channel_id=1, source_target_pairs={{0,4},{2,6},{4,0},{6,2},{8,12},{10,14},{12,8},{14,10},{16,20},{18,... | collective-permute-start | bytes 1572872 | tf_op jit(solution)/shard_map/ppermute | solution.py:166
  99.8 24.7 %collective-permute-start.14 = (bf16[4,32,2048]{2,1,0:T(8,128)(2,1)S(1)}, bf16[4,32,2048]{2,1,0:T(8,128)(2,1)S(1)}, u32[]{:S(2)}, u32[]{:S(2)}) collective-permute-start(bf16[4,32,2048]{2,1,0:T(8,128)(2,1)S(1)} %pad_maximum_fusion.7), channel_id=1, source_target_pairs={{0,2},{2,0},{4,6},{6,4},{8,10},{10,8},{12,14},{14,12},{16,18},{18,... | collective-permute-start | bytes 1572872 | tf_op jit(solution)/shard_map/ppermute | solution.py:166
  107.8 38.2 %collective-permute-start.3 = (bf16[8,32,2048]{2,1,0:T(8,128)(2,1)S(1)}, bf16[8,32,2048]{2,1,0:T(8,128)(2,1)S(1)}, u32[]{:S(2)}, u32[]{:S(2)}) collective-permute-start(bf16[8,32,2048]{2,1,0:T(8,128)(2,1)S(1)} %pad_maximum_fusion), channel_id=1, source_target_pairs={{0,2},{2,0},{4,6},{6,4},{8,10},{10,8},{12,14},{14,12},{16,18},{18,... | collective-permute-start | bytes 3145736 | tf_op jit(solution)/shard_map/ppermute | solution.py:166
  113.3 32.8 %collective-permute-start.7 = (bf16[8,32,2048]{2,1,0:T(8,128)(2,1)S(1)}, bf16[8,32,2048]{2,1,0:T(8,128)(2,1)S(1)}, u32[]{:S(2)}, u32[]{:S(2)}) collective-permute-start(bf16[8,32,2048]{2,1,0:T(8,128)(2,1)S(1)} %pad_maximum_fusion.1), channel_id=1, source_target_pairs={{0,4},{2,6},{4,0},{6,2},{8,12},{10,14},{12,8},{14,10},{16,20},{18,... | collective-permute-start | bytes 3145736 | tf_op jit(solution)/shard_map/ppermute | solution.py:166
  119.1 27.2 %collective-permute-start.11 = (bf16[8,32,2048]{2,1,0:T(8,128)(2,1)S(1)}, bf16[8,32,2048]{2,1,0:T(8,128)(2,1)S(1)}, u32[]{:S(2)}, u32[]{:S(2)}) collective-permute-start(bf16[8,32,2048]{2,1,0:T(8,128)(2,1)S(1)} %pad_maximum_fusion.2), channel_id=1, source_target_pairs={{0,8},{2,10},{4,12},{6,14},{8,0},{10,2},{12,4},{14,6},{16,24},{18,... | collective-permute-start | bytes 3145736 | tf_op jit(solution)/shard_map/ppermute | solution.py:166
  124.6 40.1 %collective-permute-start.15 = (bf16[8,32,2048]{2,1,0:T(8,128)(2,1)S(1)}, bf16[8,32,2048]{2,1,0:T(8,128)(2,1)S(1)}, u32[]{:S(2)}, u32[]{:S(2)}) collective-permute-start(bf16[8,32,2048]{2,1,0:T(8,128)(2,1)S(1)} %pad_maximum_fusion.3), channel_id=1, source_target_pairs={{0,8},{2,10},{4,12},{6,14},{8,0},{10,2},{12,4},{14,6},{16,24},{18,... | collective-permute-start | bytes 3145736 | tf_op jit(solution)/shard_map/ppermute | solution.py:166
  146.2 18.5 %copy-start.3 = (bf16[4,512,512]{2,1,0:T(8,128)(2,1)S(1)}, bf16[4,512,512]{2,1,0:T(8,128)(2,1)}, u32[]{:S(2)}) copy-start(bf16[4,512,512]{2,1,0:T(8,128)(2,1)} %constant.34.clone.g_ref) | copy-start | bytes 6291460
  146.2 18.5 %copy-start.4 = (bf16[512,256]{1,0:T(8,128)(2,1)S(1)}, bf16[512,256]{1,0:T(8,128)(2,1)}, u32[]{:S(2)}) copy-start(bf16[512,256]{1,0:T(8,128)(2,1)} %constant.33.clone.d_ref) | copy-start | bytes 786436
  146.2 18.5 %copy-start.5 = (bf16[256,256]{1,0:T(8,128)(2,1)S(1)}, bf16[256,256]{1,0:T(8,128)(2,1)}, u32[]{:S(2)}) copy-start(bf16[256,256]{1,0:T(8,128)(2,1)} %constant.35.clone.e_ref) | copy-start | bytes 393220
  279.9 1.2 collective-permute-start.16

commit v2 on v1

--- a/solution.py
+++ b/solution.py
@@ -84,7 +84,7 @@
         spec[b + NBLOCKS - 1] = dot(d_ref[:2 * SPAN], window) + dot(d_ref[2 * SPAN:], window)
         return carry
 
-    lax.fori_loop(0, steps, forward, 0)
+    lax.fori_loop(0, steps, forward, 0, unroll=4)
 
     for t in range(trials):
         taps = filters_ref[t]

time: 283 us -> 267 us (0.943)
  Pallas kernels: 115 us -> 99.8 us
    pallas_call x1, Pallas kernels: 115 us -> 99.8 us  [detect(): pl.pallas_call(functools.partial(kernel, trials, chunks), grid=(chans //...]
where the time goes in v2:
time: 267 us
  waiting for transfers between devices  122 us (46%)
  Pallas kernels  99.8 us (37%)
  starting transfers between devices  26.9 us (10%)
  local copies, waits for them, and re-layouts  8.71 us (3%)
  between operations  7.88 us (3%)
    pallas_call x1, Pallas kernels, detect(): pl.pallas_call(functools.partial(kernel, trials, chunks), grid=(chans //...  99.8 us
    ppermute x17, waiting for transfers between devices, swap(): return lax.ppermute(value, axis, [(i, i ^ 1 << bit) for i in range(size)])  86.9 us
    all_to_all x1, waiting for transfers between devices, body(): slots = lax.all_to_all(held, 'dm', 0, 0, tiled=True)  34.9 us
    ppermute x17, starting transfers between devices, swap(): return lax.ppermute(value, axis, [(i, i ^ 1 << bit) for i in range(size)])  18.4 us
    all_to_all x1, starting transfers between devices, body(): slots = lax.all_to_all(held, 'dm', 0, 0, tiled=True)  8.5 us
  transfers between devices with their start and end apart: 18, of which 14 were waited for; matrix products, arithmetic and copies ran while one was open for 1% of the time, Pallas kernels for 0%

profile of v2, /device:TPU:0, one launch (start us, length us, event | category | flops | bytes accessed | tf_op | source)
XLA Modules:
  0.0 267.1 jit_solution(17623395434183580187)
XLA Ops:
  0.0 4.1 %reshape.100 = bf16[16,32,2048]{2,1,0:T(8,128)(2,1)} reshape(bf16[1,256,2,2048]{3,2,1,0:T(2,128)(2,1)} %param.7) | data formatting | bytes 4194304 | tf_op jit(solution)/shard_map/reshape | solution.py:175
  4.1 8.5 %all-to-all-start = ((bf16[16,32,2048]{2,1,0:T(8,128)(2,1)}), bf16[16,32,2048]{2,1,0:T(8,128)(2,1)}, u32[]{:S(2)}, u32[]{:S(2)}) async-start(bf16[16,32,2048]{2,1,0:T(8,128)(2,1)} %reshape.100), calls=%async_computation | async-start | bytes 4194304 | tf_op jit(solution)/shard_map/all_to_all | solution.py:176
  12.6 0.7 fusion
  20.9 34.9 %all-to-all-done = bf16[16,32,2048]{2,1,0:T(8,128)(2,1)} async-done(((bf16[16,32,2048]{2,1,0:T(8,128)(2,1)}), bf16[16,32,2048]{2,1,0:T(8,128)(2,1)}, u32[]{:S(2)}, u32[]{:S(2)}) %all-to-all-start) | async-done | bytes 2097184 | tf_op jit(solution)/shard_map/all_to_all | solution.py:176
  55.7 1.9 constant_dynamic-update-slice_fusion.19
  57.6 7.8 %collective-permute-start = (bf16[1,32,2048]{2,1,0:T(8,128)(2,1)S(1)}, bf16[1,32,2048]{2,1,0:T(8,128)(2,1)S(1)}, u32[]{:S(2)}, u32[]{:S(2)}) collective-permute-start(bf16[1,32,2048]{2,1,0:T(8,128)(2,1)S(1)} %get-tuple-element.18), channel_id=1, source_target_pairs={{0,16},{2,18},{4,20},{6,22},{8,24},{10,26},{12,28},{14,30},{16,0},... | collective-permute-start | bytes 393224 | tf_op jit(solution)/shard_map/ppermute | solution.py:166
  65.4 0.1 dynamic_slice.15.live_ref
  65.5 0.1 collective-permute-start.4
  65.6 2.9 %collective-permute-start.8 = (bf16[1,32,2048]{2,1,0:T(8,128)(2,1)S(1)}, bf16[1,32,2048]{2,1,0:T(8,128)(2,1)S(1)}, u32[]{:S(2)}, u32[]{:S(2)}) collective-permute-start(bf16[1,32,2048]{2,1,0:T(8,128)(2,1)S(1)} %get-tuple-element.14), channel_id=1, source_target_pairs={{0,16},{2,18},{4,20},{6,22},{8,24},{10,26},{12,28},{14,30},{16,0},... | collective-permute-start | bytes 393224 | tf_op jit(solution)/shard_map/ppermute | solution.py:166
  68.5 0.1 collective-permute-start.12
  68.6 10.2 %collective-permute-done = bf16[1,32,2048]{2,1,0:T(8,128)(2,1)S(1)} collective-permute-done((bf16[1,32,2048]{2,1,0:T(8,128)(2,1)S(1)}, bf16[1,32,2048]{2,1,0:T(8,128)(2,1)S(1)}, u32[]{:S(2)}, u32[]{:S(2)}) %collective-permute-start) | collective-permute-done | bytes 131104 | tf_op jit(solution)/shard_map/ppermute | solution.py:166
  78.9 0.7 collective-permute-start.1
  79.6 2.1 collective-permute-done.4
  81.7 0.7 collective-permute-start.5
  82.4 2.2 collective-permute-done.8
  84.6 1.3 collective-permute-start.9
  85.9 1.3 collective-permute-done.12
  87.2 0.4 collective-permute-start.13
  87.6 0.7 constant_dynamic-update-slice_fusion.3
  88.3 0.6 constant_dynamic-update-slice_fusion.8
  89.0 3.8 %collective-permute-done.1 = bf16[2,32,2048]{2,1,0:T(8,128)(2,1)S(1)} collective-permute-done((bf16[2,32,2048]{2,1,0:T(8,128)(2,1)S(1)}, bf16[2,32,2048]{2,1,0:T(8,128)(2,1)S(1)}, u32[]{:S(2)}, u32[]{:S(2)}) %collective-permute-start.1) | collective-permute-done | bytes 262176 | tf_op jit(solution)/shard_map/ppermute | solution.py:166
  92.9 0.4 collective-permute-start.2
  93.3 5.1 %collective-permute-done.5 = bf16[2,32,2048]{2,1,0:T(8,128)(2,1)S(1)} collective-permute-done((bf16[2,32,2048]{2,1,0:T(8,128)(2,1)S(1)}, bf16[2,32,2048]{2,1,0:T(8,128)(2,1)S(1)}, u32[]{:S(2)}, u32[]{:S(2)}) %collective-permute-start.5) | collective-permute-done | bytes 262176 | tf_op jit(solution)/shard_map/ppermute | solution.py:166
  98.4 0.9 collective-permute-start.6
  99.3 0.4 collective-permute-start.10
  99.8 1.3 collective-permute-start.14
  101.2 6.6 %collective-permute-done.2 = bf16[4,32,2048]{2,1,0:T(8,128)(2,1)S(1)} collective-permute-done((bf16[4,32,2048]{2,1,0:T(8,128)(2,1)S(1)}, bf16[4,32,2048]{2,1,0:T(8,128)(2,1)S(1)}, u32[]{:S(2)}, u32[]{:S(2)}) %collective-permute-start.2) | collective-permute-done | bytes 524320 | tf_op jit(solution)/shard_map/ppermute | solution.py:166
  107.7 0.1 pad_maximum_fusion
  107.8 0.9 collective-permute-start.3
  108.7 4.5 %collective-permute-done.6 = bf16[4,32,2048]{2,1,0:T(8,128)(2,1)S(1)} collective-permute-done((bf16[4,32,2048]{2,1,0:T(8,128)(2,1)S(1)}, bf16[4,32,2048]{2,1,0:T(8,128)(2,1)S(1)}, u32[]{:S(2)}, u32[]{:S(2)}) %collective-permute-start.6) | collective-permute-done | bytes 524320 | tf_op jit(solution)/shard_map/ppermute | solution.py:166
  113.2 0.1 pad_maximum_fusion.1
  113.3 0.4 collective-permute-start.7
  113.7 5.2 %collective-permute-done.10 = bf16[4,32,2048]{2,1,0:T(8,128)(2,1)S(1)} collective-permute-done((bf16[4,32,2048]{2,1,0:T(8,128)(2,1)S(1)}, bf16[4,32,2048]{2,1,0:T(8,128)(2,1)S(1)}, u32[]{:S(2)}, u32[]{:S(2)}) %collective-permute-start.10) | collective-permute-done | bytes 524320 | tf_op jit(solution)/shard_map/ppermute | solution.py:166
  119.0 0.1 pad_maximum_fusion.2
  119.1 0.1 collective-permute-start.11
  119.2 5.3 %collective-permute-done.14 = bf16[4,32,2048]{2,1,0:T(8,128)(2,1)S(1)} collective-permute-done((bf16[4,32,2048]{2,1,0:T(8,128)(2,1)S(1)}, bf16[4,32,2048]{2,1,0:T(8,128)(2,1)S(1)}, u32[]{:S(2)}, u32[]{:S(2)}) %collective-permute-start.14) | collective-permute-done | bytes 524320 | tf_op jit(solution)/shard_map/ppermute | solution.py:166
  124.5 0.1 pad_maximum_fusion.3
  124.6 0.1 collective-permute-start.15
  124.8 21.1 %collective-permute-done.3 = bf16[8,32,2048]{2,1,0:T(8,128)(2,1)S(1)} collective-permute-done((bf16[8,32,2048]{2,1,0:T(8,128)(2,1)S(1)}, bf16[8,32,2048]{2,1,0:T(8,128)(2,1)S(1)}, u32[]{:S(2)}, u32[]{:S(2)}) %collective-permute-start.3) | collective-permute-done | bytes 1048608 | tf_op jit(solution)/shard_map/ppermute | solution.py:166
  146.0 0.1 constant_dynamic-update-slice_fusion.s0
  146.1 0.1 constant_dynamic-update-slice_fusion.5.s1
  146.3 0.1 constant_dynamic-update-slice_fusion.10.s2
  146.4 18.3 %collective-permute-done.15 = bf16[8,32,2048]{2,1,0:T(8,128)(2,1)S(1)} collective-permute-done((bf16[8,32,2048]{2,1,0:T(8,128)(2,1)S(1)}, bf16[8,32,2048]{2,1,0:T(8,128)(2,1)S(1)}, u32[]{:S(2)}, u32[]{:S(2)}) %collective-permute-start.15) | collective-permute-done | bytes 1048608 | tf_op jit(solution)/shard_map/ppermute | solution.py:166
  164.7 0.1 constant_dynamic-update-slice_fusion.15.s3
  164.8 99.8 %shard_map.73 = f32[2,64,2048]{2,1,0:T(8,128)S(1)} custom-call(s32[4,16]{1,0:T(4,128)S(1)} %pad_add_fusion.place_ref, s32[2]{0:T(128)S(1)} %dynamic_slice.15.live_ref, bf16[16,32,2048]{2,1,0:T(8,128)(2,1)S(1)} %constant_dynamic-update-slice_fusion.s0, bf16[16,32,2048]{2,1,0:T(8,128)(2,1)S(1)} %constant_dynamic-update-slice_fusion.5.s1, ...), custom_call_target="tpu_custom_call" | custom-call | flops 30000001024 | bytes 16000000 | tf_op jit(solution)/shard_map/pallas_call | solution.py:140
  264.6 0.1 reduce_sum.9
  264.8 1.1 collective-permute-done.16
  265.9 1.1 broadcast_divide_fusion
  (43 shorter events, 0.7 us)
Async XLA Ops:
  4.1 8.5 %copy-start.6 = (s32[4]{0:T(128)S(1)}, s32[4]{0:T(128)}, u32[]{:S(2)}) copy-start(s32[4]{0:T(128)} %param.10) | copy-start | bytes 52
  4.1 61.3 %copy-start.7 = (s32[32]{0:T(128)S(1)}, s32[32]{0:T(128)}, u32[]{:S(2)}) copy-start(s32[32]{0:T(128)} %param.9) | copy-start | bytes 388
  4.1 51.6 %all-to-all-start = ((bf16[16,32,2048]{2,1,0:T(8,128)(2,1)}), bf16[16,32,2048]{2,1,0:T(8,128)(2,1)}, u32[]{:S(2)}, u32[]{:S(2)}) async-start(bf16[16,32,2048]{2,1,0:T(8,128)(2,1)} %reshape.100), calls=%async_computation | async-start | bytes 4194304 | tf_op jit(solution)/shard_map/all_to_all | solution.py:176
  57.6 21.2 %collective-permute-start = (bf16[1,32,2048]{2,1,0:T(8,128)(2,1)S(1)}, bf16[1,32,2048]{2,1,0:T(8,128)(2,1)S(1)}, u32[]{:S(2)}, u32[]{:S(2)}) collective-permute-start(bf16[1,32,2048]{2,1,0:T(8,128)(2,1)S(1)} %get-tuple-element.18), channel_id=1, source_target_pairs={{0,16},{2,18},{4,20},{6,22},{8,24},{10,26},{12,28},{14,30},{16,0},... | collective-permute-start | bytes 393224 | tf_op jit(solution)/shard_map/ppermute | solution.py:166
  65.4 23.5 %copy-start = (bf16[16,32,2048]{2,1,0:T(8,128)(2,1)S(1)}, bf16[16,32,2048]{2,1,0:T(8,128)(2,1)}, u32[]{:S(2)}) copy-start(bf16[16,32,2048]{2,1,0:T(8,128)(2,1)} %get-tuple-element.13) | copy-start | bytes 6291460
  65.5 16.2 %collective-permute-start.4 = (bf16[1,32,2048]{2,1,0:T(8,128)(2,1)S(1)}, bf16[1,32,2048]{2,1,0:T(8,128)(2,1)S(1)}, u32[]{:S(2)}, u32[]{:S(2)}) collective-permute-start(bf16[1,32,2048]{2,1,0:T(8,128)(2,1)S(1)} %get-tuple-element.16), channel_id=1, source_target_pairs={{0,16},{2,18},{4,20},{6,22},{8,24},{10,26},{12,28},{14,30},{16,0},... | collective-permute-start | bytes 393224 | tf_op jit(solution)/shard_map/ppermute | solution.py:166
  65.6 19.0 %collective-permute-start.8 = (bf16[1,32,2048]{2,1,0:T(8,128)(2,1)S(1)}, bf16[1,32,2048]{2,1,0:T(8,128)(2,1)S(1)}, u32[]{:S(2)}, u32[]{:S(2)}) collective-permute-start(bf16[1,32,2048]{2,1,0:T(8,128)(2,1)S(1)} %get-tuple-element.14), channel_id=1, source_target_pairs={{0,16},{2,18},{4,20},{6,22},{8,24},{10,26},{12,28},{14,30},{16,0},... | collective-permute-start | bytes 393224 | tf_op jit(solution)/shard_map/ppermute | solution.py:166
  68.5 18.7 %collective-permute-start.12 = (bf16[1,32,2048]{2,1,0:T(8,128)(2,1)S(1)}, bf16[1,32,2048]{2,1,0:T(8,128)(2,1)S(1)}, u32[]{:S(2)}, u32[]{:S(2)}) collective-permute-start(bf16[1,32,2048]{2,1,0:T(8,128)(2,1)S(1)} %get-tuple-element.6), channel_id=1, source_target_pairs={{0,16},{2,18},{4,20},{6,22},{8,24},{10,26},{12,28},{14,30},{16,0},... | collective-permute-start | bytes 393224 | tf_op jit(solution)/shard_map/ppermute | solution.py:166
  78.9 13.9 %collective-permute-start.1 = (bf16[2,32,2048]{2,1,0:T(8,128)(2,1)S(1)}, bf16[2,32,2048]{2,1,0:T(8,128)(2,1)S(1)}, u32[]{:S(2)}, u32[]{:S(2)}) collective-permute-start(bf16[2,32,2048]{2,1,0:T(8,128)(2,1)S(1)} %pad_maximum_fusion.8), channel_id=1, source_target_pairs={{0,8},{2,10},{4,12},{6,14},{8,0},{10,2},{12,4},{14,6},{16,24},{18,... | collective-permute-start | bytes 786440 | tf_op jit(solution)/shard_map/ppermute | solution.py:166
  81.7 16.6 %collective-permute-start.5 = (bf16[2,32,2048]{2,1,0:T(8,128)(2,1)S(1)}, bf16[2,32,2048]{2,1,0:T(8,128)(2,1)S(1)}, u32[]{:S(2)}, u32[]{:S(2)}) collective-permute-start(bf16[2,32,2048]{2,1,0:T(8,128)(2,1)S(1)} %pad_maximum_fusion.9), channel_id=1, source_target_pairs={{0,8},{2,10},{4,12},{6,14},{8,0},{10,2},{12,4},{14,6},{16,24},{18,... | collective-permute-start | bytes 786440 | tf_op jit(solution)/shard_map/ppermute | solution.py:166
  84.6 14.7 %collective-permute-start.9 = (bf16[2,32,2048]{2,1,0:T(8,128)(2,1)S(1)}, bf16[2,32,2048]{2,1,0:T(8,128)(2,1)S(1)}, u32[]{:S(2)}, u32[]{:S(2)}) collective-permute-start(bf16[2,32,2048]{2,1,0:T(8,128)(2,1)S(1)} %pad_maximum_fusion.10), channel_id=1, source_target_pairs={{0,2},{2,0},{4,6},{6,4},{8,10},{10,8},{12,14},{14,12},{16,18},{18,... | collective-permute-start | bytes 786440 | tf_op jit(solution)/shard_map/ppermute | solution.py:166
  87.2 12.5 %collective-permute-start.13 = (bf16[2,32,2048]{2,1,0:T(8,128)(2,1)S(1)}, bf16[2,32,2048]{2,1,0:T(8,128)(2,1)S(1)}, u32[]{:S(2)}, u32[]{:S(2)}) collective-permute-start(bf16[2,32,2048]{2,1,0:T(8,128)(2,1)S(1)} %pad_maximum_fusion.11), channel_id=1, source_target_pairs={{0,4},{2,6},{4,0},{6,2},{8,12},{10,14},{12,8},{14,10},{16,20},{18,... | collective-permute-start | bytes 786440 | tf_op jit(solution)/shard_map/ppermute | solution.py:166
  89.0 12.1 %copy-start.2 = (bf16[16,32,2048]{2,1,0:T(8,128)(2,1)S(1)}, bf16[16,32,2048]{2,1,0:T(8,128)(2,1)}, u32[]{:S(2)}) copy-start(bf16[16,32,2048]{2,1,0:T(8,128)(2,1)} %constant_dynamic-update-slice_fusion.3) | copy-start | bytes 6291460
  92.9 8.2 %copy-start.1 = (bf16[16,32,2048]{2,1,0:T(8,128)(2,1)S(1)}, bf16[16,32,2048]{2,1,0:T(8,128)(2,1)}, u32[]{:S(2)}) copy-start(bf16[16,32,2048]{2,1,0:T(8,128)(2,1)} %constant_dynamic-update-slice_fusion.8) | copy-start | bytes 6291460
  92.9 14.9 %collective-permute-start.2 = (bf16[4,32,2048]{2,1,0:T(8,128)(2,1)S(1)}, bf16[4,32,2048]{2,1,0:T(8,128)(2,1)S(1)}, u32[]{:S(2)}, u32[]{:S(2)}) collective-permute-start(bf16[4,32,2048]{2,1,0:T(8,128)(2,1)S(1)} %pad_maximum_fusion.4), channel_id=1, source_target_pairs={{0,4},{2,6},{4,0},{6,2},{8,12},{10,14},{12,8},{14,10},{16,20},{18,... | collective-permute-start | bytes 1572872 | tf_op jit(solution)/shard_map/ppermute | solution.py:166
  98.4 14.8 %collective-permute-start.6 = (bf16[4,32,2048]{2,1,0:T(8,128)(2,1)S(1)}, bf16[4,32,2048]{2,1,0:T(8,128)(2,1)S(1)}, u32[]{:S(2)}, u32[]{:S(2)}) collective-permute-start(bf16[4,32,2048]{2,1,0:T(8,128)(2,1)S(1)} %pad_maximum_fusion.5), channel_id=1, source_target_pairs={{0,2},{2,0},{4,6},{6,4},{8,10},{10,8},{12,14},{14,12},{16,18},{18,... | collective-permute-start | bytes 1572872 | tf_op jit(solution)/shard_map/ppermute | solution.py:166
  99.3 19.7 %collective-permute-start.10 = (bf16[4,32,2048]{2,1,0:T(8,128)(2,1)S(1)}, bf16[4,32,2048]{2,1,0:T(8,128)(2,1)S(1)}, u32[]{:S(2)}, u32[]{:S(2)}) collective-permute-start(bf16[4,32,2048]{2,1,0:T(8,128)(2,1)S(1)} %pad_maximum_fusion.6), channel_id=1, source_target_pairs={{0,4},{2,6},{4,0},{6,2},{8,12},{10,14},{12,8},{14,10},{16,20},{18,... | collective-permute-start | bytes 1572872 | tf_op jit(solution)/shard_map/ppermute | solution.py:166
  99.8 24.7 %collective-permute-start.14 = (bf16[4,32,2048]{2,1,0:T(8,128)(2,1)S(1)}, bf16[4,32,2048]{2,1,0:T(8,128)(2,1)S(1)}, u32[]{:S(2)}, u32[]{:S(2)}) collective-permute-start(bf16[4,32,2048]{2,1,0:T(8,128)(2,1)S(1)} %pad_maximum_fusion.7), channel_id=1, source_target_pairs={{0,2},{2,0},{4,6},{6,4},{8,10},{10,8},{12,14},{14,12},{16,18},{18,... | collective-permute-start | bytes 1572872 | tf_op jit(solution)/shard_map/ppermute | solution.py:166
  107.8 38.2 %collective-permute-start.3 = (bf16[8,32,2048]{2,1,0:T(8,128)(2,1)S(1)}, bf16[8,32,2048]{2,1,0:T(8,128)(2,1)S(1)}, u32[]{:S(2)}, u32[]{:S(2)}) collective-permute-start(bf16[8,32,2048]{2,1,0:T(8,128)(2,1)S(1)} %pad_maximum_fusion), channel_id=1, source_target_pairs={{0,2},{2,0},{4,6},{6,4},{8,10},{10,8},{12,14},{14,12},{16,18},{18,... | collective-permute-start | bytes 3145736 | tf_op jit(solution)/shard_map/ppermute | solution.py:166
  113.3 32.8 %collective-permute-start.7 = (bf16[8,32,2048]{2,1,0:T(8,128)(2,1)S(1)}, bf16[8,32,2048]{2,1,0:T(8,128)(2,1)S(1)}, u32[]{:S(2)}, u32[]{:S(2)}) collective-permute-start(bf16[8,32,2048]{2,1,0:T(8,128)(2,1)S(1)} %pad_maximum_fusion.1), channel_id=1, source_target_pairs={{0,4},{2,6},{4,0},{6,2},{8,12},{10,14},{12,8},{14,10},{16,20},{18,... | collective-permute-start | bytes 3145736 | tf_op jit(solution)/shard_map/ppermute | solution.py:166
  119.1 27.2 %collective-permute-start.11 = (bf16[8,32,2048]{2,1,0:T(8,128)(2,1)S(1)}, bf16[8,32,2048]{2,1,0:T(8,128)(2,1)S(1)}, u32[]{:S(2)}, u32[]{:S(2)}) collective-permute-start(bf16[8,32,2048]{2,1,0:T(8,128)(2,1)S(1)} %pad_maximum_fusion.2), channel_id=1, source_target_pairs={{0,8},{2,10},{4,12},{6,14},{8,0},{10,2},{12,4},{14,6},{16,24},{18,... | collective-permute-start | bytes 3145736 | tf_op jit(solution)/shard_map/ppermute | solution.py:166
  124.6 40.1 %collective-permute-start.15 = (bf16[8,32,2048]{2,1,0:T(8,128)(2,1)S(1)}, bf16[8,32,2048]{2,1,0:T(8,128)(2,1)S(1)}, u32[]{:S(2)}, u32[]{:S(2)}) collective-permute-start(bf16[8,32,2048]{2,1,0:T(8,128)(2,1)S(1)} %pad_maximum_fusion.3), channel_id=1, source_target_pairs={{0,8},{2,10},{4,12},{6,14},{8,0},{10,2},{12,4},{14,6},{16,24},{18,... | collective-permute-start | bytes 3145736 | tf_op jit(solution)/shard_map/ppermute | solution.py:166
  146.2 18.5 %copy-start.3 = (bf16[4,512,512]{2,1,0:T(8,128)(2,1)S(1)}, bf16[4,512,512]{2,1,0:T(8,128)(2,1)}, u32[]{:S(2)}) copy-start(bf16[4,512,512]{2,1,0:T(8,128)(2,1)} %constant.34.clone.g_ref) | copy-start | bytes 6291460
  146.2 18.5 %copy-start.4 = (bf16[512,256]{1,0:T(8,128)(2,1)S(1)}, bf16[512,256]{1,0:T(8,128)(2,1)}, u32[]{:S(2)}) copy-start(bf16[512,256]{1,0:T(8,128)(2,1)} %constant.33.clone.d_ref) | copy-start | bytes 786436
  146.2 18.5 %copy-start.5 = (bf16[256,256]{1,0:T(8,128)(2,1)S(1)}, bf16[256,256]{1,0:T(8,128)(2,1)}, u32[]{:S(2)}) copy-start(bf16[256,256]{1,0:T(8,128)(2,1)} %constant.35.clone.e_ref) | copy-start | bytes 393220
  264.7 1.2 collective-permute-start.16
